TPU v7x, 512 devices: a whole 4x8x8 slice. The times are simulated.
512 devices in a mesh: freq: 32 (over x, z_lo, core), tile: 16 (over y, z_hi).
Axes of the slice: x: 4, y: 8, z: 8 (z_hi: 2, z_lo: 4; z = z_hi * 4 + z_lo), core: 2. Of those that a mesh axis runs over, the one named last changes fastest.
Arguments:
- source_field: float32 [2, 32, 256, 1024], P(None, 'freq', 'tile'), may hold values from -6 to 6
- receiver_field: float32 [2, 32, 256, 1024], P(None, 'freq', 'tile'), may hold values from -6 to 6
- velocity_store: float32 [32, 256, 1024], P('freq', 'tile'), may hold values from 0.5 to 1
- slice_owner: int32 [4], replicated, may hold values from 0 to 31, as said below
- region_map: int32 [256, 1024], P('tile', 'freq'), may hold values from 0 to 3, as said below
Outputs:
- wavefields: float32 [2, 2, 32, 256, 1024], P(None, None, 'freq', 'tile')
- smoothed_image: float32 [4, 256, 1024], P(None, 'tile', 'freq')
Inputs may be any that keep to these rules, and one draw needn't show every extreme that they name: `slice_owner`: the 4 entries are distinct stored-slice indices; slices 0 and 31 are always among them. `region_map`: labels along the second lateral dimension change at scattered cells.
All inputs are finite; a program needn't handle non-finite values.
Results may differ from a plain program's by a relative error of at most 0.000023.
Values sent between devices are 32-bit elements; how exact they have to be, the bound alone decides.
A program may use at most 64 MiB of HBM per device.

v0:
```python
import math

import jax
import jax.numpy as jnp
from jax import lax
from jax.sharding import PartitionSpec as P

SWEEPS = 3


DAMPING = 0.125
ROTATION = 0.125
STEP_DEPTH = 4.0
SMOOTHING = 0.25


def from_root(block, axis, source):
    block = jnp.where(lax.axis_index(axis) == source, block, jnp.zeros_like(block))
    return lax.psum(block, axis)


def extended(block, sides, width):
    for axis, dim in sides:
        count = lax.axis_size(axis)
        forward = [(i, i + 1) for i in range(count - 1)]
        backward = [(target, source) for source, target in forward]
        low = lax.ppermute(
            lax.slice_in_dim(block, block.shape[dim] - width, None, axis=dim), axis, forward
        )
        high = lax.ppermute(lax.slice_in_dim(block, 0, width, axis=dim), axis, backward)
        block = jnp.concatenate([low, block, high], axis=dim)
    return block


def laplace_rows(padded):
    center = padded[..., 1:-1, :]
    beside_x = padded[..., 2:, :] + padded[..., :-2, :]
    widths = [(0, 0)] * (center.ndim - 1) + [(1, 1)]
    sided = jnp.pad(center, widths)
    beside_y = sided[..., 2:] + sided[..., :-2]
    return (center, beside_x + beside_y - 4.0 * center)


def advance(padded, signed):
    center, spread = laplace_rows(padded)
    real_part = center[:, 0] + DAMPING * spread[:, 0] - signed * spread[:, 1]
    imag_part = center[:, 1] + DAMPING * spread[:, 1] + signed * spread[:, 0]
    return jnp.stack([real_part, imag_part], axis=1)


def on_device(source_field, receiver_field, velocity_store, slice_owner, region_map):
    freq_local = source_field.shape[1]
    total_freqs = freq_local * lax.axis_size("freq")
    first_freq = lax.axis_index("freq") * freq_local
    omegas = (
        1.0
        + (first_freq + jnp.arange(freq_local, dtype=jnp.int32)).astype(jnp.float32) / total_freqs
    )
    fields = jnp.stack([source_field, receiver_field])
    depth_count = slice_owner.shape[0]
    pieces = []
    for depth_no in range(depth_count):
        speed_map = from_root(velocity_store[0], "freq", slice_owner[depth_no])
        angles = omegas[:, None, None] * STEP_DEPTH / speed_map[None]
        cosines = jnp.cos(angles)
        sines = jnp.sin(angles)
        negated = -sines
        source_now = jnp.stack(
            [
                fields[0, 0] * cosines - fields[0, 1] * sines,
                fields[0, 0] * sines + fields[0, 1] * cosines,
            ]
        )
        receiver_now = jnp.stack(
            [
                fields[1, 0] * cosines - fields[1, 1] * negated,
                fields[1, 0] * negated + fields[1, 1] * cosines,
            ]
        )
        fields = jnp.stack([source_now, receiver_now])
        coeff = ROTATION * speed_map[None] / omegas[:, None, None]
        signed = jnp.stack([coeff, -coeff])
        for sweep_no in range(SWEEPS):
            padded = extended(fields, (("tile", 3),), 1)
            fields = advance(padded, signed)
        layer_term = jnp.sum(fields[0, 0] * fields[1, 0] + fields[0, 1] * fields[1, 1], axis=0)
        pieces.append(layer_term)
    image_sum = lax.psum_scatter(jnp.stack(pieces), "freq", scatter_dimension=2, tiled=True)
    image_sum = image_sum / math.sqrt(total_freqs)
    labels = region_map.astype(jnp.float32) + 1.0
    stacked = jnp.concatenate([image_sum, labels[None]], axis=0)
    padded = extended(stacked, (("freq", 2),), 1)
    image_pad = padded[:depth_count]
    label_pad = padded[depth_count]
    label_mid = label_pad[:, 1:-1]
    next_same = (label_pad[:, 2:] == label_mid).astype(jnp.float32)
    prev_same = (label_pad[:, :-2] == label_mid).astype(jnp.float32)
    smoothed = image_sum + SMOOTHING * (
        next_same * (image_pad[..., 2:] - image_sum) + prev_same * (image_pad[..., :-2] - image_sum)
    )
    return (fields, smoothed)


def solution(mesh):
    in_specs = (
        P(None, "freq", "tile", None),
        P(None, "freq", "tile", None),
        P("freq", "tile", None),
        P(),
        P("tile", "freq"),
    )
    out_specs = (P(None, None, "freq", "tile", None), P(None, "tile", "freq"))
    return jax.shard_map(
        on_device, mesh=mesh, in_specs=in_specs, out_specs=out_specs, check_vma=False
    )
```

profile of v0, /device:TPU:1, one launch (start us, length us, event | category | flops | bytes accessed | tf_op | source)
XLA Modules:
  0.0 647.1 jit_solution(6522932462620739825)
XLA Ops:
  7.2 1.5 fusion.180
  11.2 1.5 select_bitcast_fusion
  12.9 286.5 %all-reduce.15.cloned.1.call-done = (f32[16,1024]{1,0:T(8,128)}, f32[16,1024]{1,0:T(8,128)}, f32[16,1024]{1,0:T(8,128)}, f32[16,1024]{1,0:T(8,128)}) async-done(((f32[16,1024]{1,0:T(8,128)}, f32[16,1024]{1,0:T(8,128)}, f32[16,1024]{1,0:T(8,128)}, f32[16,1024]{1,0:T(8,128)}), (f32[16,1024]{1,0:T(8,128)}, f32[16,1024]{1,0:T(8,128)}, f32[16,1024]{1,0:T(8,128)}, ...) | async-done | bytes 262160 | tf_op jit(solution)/shard_map/psum | solution.py:19
  300.7 5.0 collective-permute-start.1
  307.1 7.1 %collective-permute-done = f32[2,2,1,1,1024]{4,3,0,2,1:T(1,128)S(1)} collective-permute-done((f32[2,2,1,1,1024]{4,3,0,2,1:T(1,128)S(1)}, f32[2,2,1,1,1024]{4,3,0,2,1:T(1,128)S(1)}, u32[]{:S(2)}, u32[]{:S(2)}) %collective-permute-start) | collective-permute-done | bytes 16416 | tf_op jit(solution)/shard_map/ppermute | solution.py:30
  314.4 6.0 collective-permute-start.3
  321.8 7.1 %collective-permute-done.2 = f32[2,2,1,1,1024]{4,3,0,2,1:T(1,128)S(1)} collective-permute-done((f32[2,2,1,1,1024]{4,3,0,2,1:T(1,128)S(1)}, f32[2,2,1,1,1024]{4,3,0,2,1:T(1,128)S(1)}, u32[]{:S(2)}, u32[]{:S(2)}) %collective-permute-start.2) | collective-permute-done | bytes 16416 | tf_op jit(solution)/shard_map/ppermute | solution.py:30
  329.1 5.0 collective-permute-start.5
  335.5 7.1 %collective-permute-done.4 = f32[2,2,1,1,1024]{4,3,0,2,1:T(1,128)S(1)} collective-permute-done((f32[2,2,1,1,1024]{4,3,0,2,1:T(1,128)S(1)}, f32[2,2,1,1,1024]{4,3,0,2,1:T(1,128)S(1)}, u32[]{:S(2)}, u32[]{:S(2)}) %collective-permute-start.4) | collective-permute-done | bytes 16416 | tf_op jit(solution)/shard_map/ppermute | solution.py:30
  343.3 6.0 collective-permute-start.7
  350.6 7.1 %collective-permute-done.6 = f32[2,2,1,1,1024]{4,3,0,2,1:T(1,128)S(1)} collective-permute-done((f32[2,2,1,1,1024]{4,3,0,2,1:T(1,128)S(1)}, f32[2,2,1,1,1024]{4,3,0,2,1:T(1,128)S(1)}, u32[]{:S(2)}, u32[]{:S(2)}) %collective-permute-start.6) | collective-permute-done | bytes 16416 | tf_op jit(solution)/shard_map/ppermute | solution.py:30
  358.0 5.0 collective-permute-start.9
  364.4 7.1 %collective-permute-done.8 = f32[2,2,1,1,1024]{4,3,0,2,1:T(1,128)S(1)} collective-permute-done((f32[2,2,1,1,1024]{4,3,0,2,1:T(1,128)S(1)}, f32[2,2,1,1,1024]{4,3,0,2,1:T(1,128)S(1)}, u32[]{:S(2)}, u32[]{:S(2)}) %collective-permute-start.8) | collective-permute-done | bytes 16416 | tf_op jit(solution)/shard_map/ppermute | solution.py:30
  371.7 6.0 collective-permute-start.11
  377.7 1.3 collective-permute-start.10
  379.1 7.0 %collective-permute-done.10 = f32[2,2,1,1,1024]{4,3,0,2,1:T(1,128)S(1)} collective-permute-done((f32[2,2,1,1,1024]{4,3,0,2,1:T(1,128)S(1)}, f32[2,2,1,1,1024]{4,3,0,2,1:T(1,128)S(1)}, u32[]{:S(2)}, u32[]{:S(2)}) %collective-permute-start.10) | collective-permute-done | bytes 16416 | tf_op jit(solution)/shard_map/ppermute | solution.py:30
  386.9 5.3 collective-permute-start.13
  393.5 7.1 %collective-permute-done.12 = f32[2,2,1,1,1024]{4,3,0,2,1:T(1,128)S(1)} collective-permute-done((f32[2,2,1,1,1024]{4,3,0,2,1:T(1,128)S(1)}, f32[2,2,1,1,1024]{4,3,0,2,1:T(1,128)S(1)}, u32[]{:S(2)}, u32[]{:S(2)}) %collective-permute-start.12) | collective-permute-done | bytes 16416 | tf_op jit(solution)/shard_map/ppermute | solution.py:30
  400.8 8.2 %collective-permute-start.15 = (f32[2,2,1,1,1024]{4,3,0,2,1:T(1,128)S(1)}, f32[2,2,1,1,1024]{4,3,0,2,1:T(1,128)S(1)}, u32[]{:S(2)}, u32[]{:S(2)}) collective-permute-start(f32[2,2,1,1,1024]{4,3,0,2,1:T(1,128)S(1)} %get-tuple-element.49), channel_id=1, source_target_pairs={{0,1},{1,2},{2,3},{3,4},{4,5},{5,6},{6,7},{7,8},{8,9},{9,10},{10,1... | collective-permute-start | bytes 49160 | tf_op jit(solution)/shard_map/ppermute | solution.py:27
  410.3 7.1 %collective-permute-done.14 = f32[2,2,1,1,1024]{4,3,0,2,1:T(1,128)S(1)} collective-permute-done((f32[2,2,1,1,1024]{4,3,0,2,1:T(1,128)S(1)}, f32[2,2,1,1,1024]{4,3,0,2,1:T(1,128)S(1)}, u32[]{:S(2)}, u32[]{:S(2)}) %collective-permute-start.14) | collective-permute-done | bytes 16416 | tf_op jit(solution)/shard_map/ppermute | solution.py:30
  417.7 5.2 collective-permute-start.17
  424.3 7.1 %collective-permute-done.16 = f32[2,2,1,1,1024]{4,3,0,2,1:T(1,128)S(1)} collective-permute-done((f32[2,2,1,1,1024]{4,3,0,2,1:T(1,128)S(1)}, f32[2,2,1,1,1024]{4,3,0,2,1:T(1,128)S(1)}, u32[]{:S(2)}, u32[]{:S(2)}) %collective-permute-start.16) | collective-permute-done | bytes 16416 | tf_op jit(solution)/shard_map/ppermute | solution.py:30
  432.1 4.9 collective-permute-start.19
  438.3 7.1 %collective-permute-done.18 = f32[2,2,1,1,1024]{4,3,0,2,1:T(1,128)S(1)} collective-permute-done((f32[2,2,1,1,1024]{4,3,0,2,1:T(1,128)S(1)}, f32[2,2,1,1,1024]{4,3,0,2,1:T(1,128)S(1)}, u32[]{:S(2)}, u32[]{:S(2)}) %collective-permute-start.18) | collective-permute-done | bytes 16416 | tf_op jit(solution)/shard_map/ppermute | solution.py:30
  445.7 5.1 collective-permute-start.21
  452.2 7.1 %collective-permute-done.20 = f32[2,2,1,1,1024]{4,3,0,2,1:T(1,128)S(1)} collective-permute-done((f32[2,2,1,1,1024]{4,3,0,2,1:T(1,128)S(1)}, f32[2,2,1,1,1024]{4,3,0,2,1:T(1,128)S(1)}, u32[]{:S(2)}, u32[]{:S(2)}) %collective-permute-start.20) | collective-permute-done | bytes 16416 | tf_op jit(solution)/shard_map/ppermute | solution.py:30
  459.5 5.6 collective-permute-start.23
  466.4 7.1 %collective-permute-done.22 = f32[2,2,1,1,1024]{4,3,0,2,1:T(1,128)S(1)} collective-permute-done((f32[2,2,1,1,1024]{4,3,0,2,1:T(1,128)S(1)}, f32[2,2,1,1,1024]{4,3,0,2,1:T(1,128)S(1)}, u32[]{:S(2)}, u32[]{:S(2)}) %collective-permute-start.22) | collective-permute-done | bytes 16416 | tf_op jit(solution)/shard_map/ppermute | solution.py:30
  474.8 1.7 reshape.2659
  476.6 152.3 %reduce-scatter.4.cloned.1.call-done = f32[32,64]{1,0:T(8,128)} async-done(((f32[1024,64]{1,0:T(8,128)}), f32[32,64]{1,0:T(8,128)}) %reduce-scatter.4.cloned.1.call-update) | async-done | bytes 8208
  629.9 2.8 collective-permute-start.24
  632.7 5.9 collective-permute-start.25
  (116 shorter events, 24.2 us)
Async XLA Ops:
  7.2 292.2 %all-reduce.15.cloned.1.call-start = ((), (), s32[]{:S(2)}) async-start(), calls=%async_computation.2 | async-start | bytes 524288 | tf_op jit(solution)/shard_map/psum | solution.py:19
  12.8 616.1 %reduce-scatter.4.cloned.1.call-start = ((), (), s32[]{:S(2)}) async-start(), calls=%async_computation.1 | async-start | bytes 540672
  300.7 6.4 collective-permute-start.1
  305.7 8.4 %collective-permute-start = (f32[2,2,1,1,1024]{4,3,0,2,1:T(1,128)S(1)}, f32[2,2,1,1,1024]{4,3,0,2,1:T(1,128)S(1)}, u32[]{:S(2)}, u32[]{:S(2)}) collective-permute-start(f32[2,2,1,1,1024]{4,3,0,2,1:T(1,128)S(1)} %get-tuple-element.62), channel_id=1, source_target_pairs={{1,0},{2,1},{3,2},{4,3},{5,4},{6,5},{7,6},{8,7},{9,8},{10,9},{11,1... | collective-permute-start | bytes 49160 | tf_op jit(solution)/shard_map/ppermute | solution.py:30
  314.4 7.3 %collective-permute-start.3 = (f32[2,2,1,1,1024]{4,3,0,2,1:T(1,128)S(1)}, f32[2,2,1,1,1024]{4,3,0,2,1:T(1,128)S(1)}, u32[]{:S(2)}, u32[]{:S(2)}) collective-permute-start(f32[2,2,1,1,1024]{4,3,0,2,1:T(1,128)S(1)} %get-tuple-element.61), channel_id=1, source_target_pairs={{0,1},{1,2},{2,3},{3,4},{4,5},{5,6},{6,7},{7,8},{8,9},{9,10},{10,1... | collective-permute-start | bytes 49160 | tf_op jit(solution)/shard_map/ppermute | solution.py:27
  320.4 8.4 %collective-permute-start.2 = (f32[2,2,1,1,1024]{4,3,0,2,1:T(1,128)S(1)}, f32[2,2,1,1,1024]{4,3,0,2,1:T(1,128)S(1)}, u32[]{:S(2)}, u32[]{:S(2)}) collective-permute-start(f32[2,2,1,1,1024]{4,3,0,2,1:T(1,128)S(1)} %get-tuple-element.60), channel_id=1, source_target_pairs={{1,0},{2,1},{3,2},{4,3},{5,4},{6,5},{7,6},{8,7},{9,8},{10,9},{11,1... | collective-permute-start | bytes 49160 | tf_op jit(solution)/shard_map/ppermute | solution.py:30
  329.1 13.8 %copy-start.2 = (f32[16,1024]{1,0:T(8,128)S(1)}, f32[16,1024]{1,0:T(8,128)}, u32[]{:S(2)}) copy-start(f32[16,1024]{1,0:T(8,128)} %get-tuple-element.7) | copy-start | bytes 196612
  329.1 6.4 collective-permute-start.5
  334.2 8.4 %collective-permute-start.4 = (f32[2,2,1,1,1024]{4,3,0,2,1:T(1,128)S(1)}, f32[2,2,1,1,1024]{4,3,0,2,1:T(1,128)S(1)}, u32[]{:S(2)}, u32[]{:S(2)}) collective-permute-start(f32[2,2,1,1,1024]{4,3,0,2,1:T(1,128)S(1)} %get-tuple-element.58), channel_id=1, source_target_pairs={{1,0},{2,1},{3,2},{4,3},{5,4},{6,5},{7,6},{8,7},{9,8},{10,9},{11,1... | collective-permute-start | bytes 49160 | tf_op jit(solution)/shard_map/ppermute | solution.py:30
  343.3 7.4 %collective-permute-start.7 = (f32[2,2,1,1,1024]{4,3,0,2,1:T(1,128)S(1)}, f32[2,2,1,1,1024]{4,3,0,2,1:T(1,128)S(1)}, u32[]{:S(2)}, u32[]{:S(2)}) collective-permute-start(f32[2,2,1,1,1024]{4,3,0,2,1:T(1,128)S(1)} %get-tuple-element.57), channel_id=1, source_target_pairs={{0,1},{1,2},{2,3},{3,4},{4,5},{5,6},{6,7},{7,8},{8,9},{9,10},{10,1... | collective-permute-start | bytes 49160 | tf_op jit(solution)/shard_map/ppermute | solution.py:27
  349.3 8.4 %collective-permute-start.6 = (f32[2,2,1,1,1024]{4,3,0,2,1:T(1,128)S(1)}, f32[2,2,1,1,1024]{4,3,0,2,1:T(1,128)S(1)}, u32[]{:S(2)}, u32[]{:S(2)}) collective-permute-start(f32[2,2,1,1,1024]{4,3,0,2,1:T(1,128)S(1)} %get-tuple-element.56), channel_id=1, source_target_pairs={{1,0},{2,1},{3,2},{4,3},{5,4},{6,5},{7,6},{8,7},{9,8},{10,9},{11,1... | collective-permute-start | bytes 49160 | tf_op jit(solution)/shard_map/ppermute | solution.py:30
  358.0 6.4 collective-permute-start.9
  363.0 8.4 %collective-permute-start.8 = (f32[2,2,1,1,1024]{4,3,0,2,1:T(1,128)S(1)}, f32[2,2,1,1,1024]{4,3,0,2,1:T(1,128)S(1)}, u32[]{:S(2)}, u32[]{:S(2)}) collective-permute-start(f32[2,2,1,1,1024]{4,3,0,2,1:T(1,128)S(1)} %get-tuple-element.54), channel_id=1, source_target_pairs={{1,0},{2,1},{3,2},{4,3},{5,4},{6,5},{7,6},{8,7},{9,8},{10,9},{11,1... | collective-permute-start | bytes 49160 | tf_op jit(solution)/shard_map/ppermute | solution.py:30
  371.7 7.3 %collective-permute-start.11 = (f32[2,2,1,1,1024]{4,3,0,2,1:T(1,128)S(1)}, f32[2,2,1,1,1024]{4,3,0,2,1:T(1,128)S(1)}, u32[]{:S(2)}, u32[]{:S(2)}) collective-permute-start(f32[2,2,1,1,1024]{4,3,0,2,1:T(1,128)S(1)} %get-tuple-element.53), channel_id=1, source_target_pairs={{0,1},{1,2},{2,3},{3,4},{4,5},{5,6},{6,7},{7,8},{8,9},{9,10},{10,1... | collective-permute-start | bytes 49160 | tf_op jit(solution)/shard_map/ppermute | solution.py:27
  377.7 8.4 %collective-permute-start.10 = (f32[2,2,1,1,1024]{4,3,0,2,1:T(1,128)S(1)}, f32[2,2,1,1,1024]{4,3,0,2,1:T(1,128)S(1)}, u32[]{:S(2)}, u32[]{:S(2)}) collective-permute-start(f32[2,2,1,1,1024]{4,3,0,2,1:T(1,128)S(1)} %get-tuple-element.52), channel_id=1, source_target_pairs={{1,0},{2,1},{3,2},{4,3},{5,4},{6,5},{7,6},{8,7},{9,8},{10,9},{11,1... | collective-permute-start | bytes 49160 | tf_op jit(solution)/shard_map/ppermute | solution.py:30
  379.0 7.5 %copy-start.1 = (f32[16,1024]{1,0:T(8,128)S(1)}, f32[16,1024]{1,0:T(8,128)}, u32[]{:S(2)}) copy-start(f32[16,1024]{1,0:T(8,128)} %get-tuple-element.8) | copy-start | bytes 196612
  386.9 6.6 %collective-permute-start.13 = (f32[2,2,1,1,1024]{4,3,0,2,1:T(1,128)S(1)}, f32[2,2,1,1,1024]{4,3,0,2,1:T(1,128)S(1)}, u32[]{:S(2)}, u32[]{:S(2)}) collective-permute-start(f32[2,2,1,1,1024]{4,3,0,2,1:T(1,128)S(1)} %get-tuple-element.51), channel_id=1, source_target_pairs={{0,1},{1,2},{2,3},{3,4},{4,5},{5,6},{6,7},{7,8},{8,9},{9,10},{10,1... | collective-permute-start | bytes 49160 | tf_op jit(solution)/shard_map/ppermute | solution.py:27
  392.2 8.4 %collective-permute-start.12 = (f32[2,2,1,1,1024]{4,3,0,2,1:T(1,128)S(1)}, f32[2,2,1,1,1024]{4,3,0,2,1:T(1,128)S(1)}, u32[]{:S(2)}, u32[]{:S(2)}) collective-permute-start(f32[2,2,1,1,1024]{4,3,0,2,1:T(1,128)S(1)} %get-tuple-element.50), channel_id=1, source_target_pairs={{1,0},{2,1},{3,2},{4,3},{5,4},{6,5},{7,6},{8,7},{9,8},{10,9},{11,1... | collective-permute-start | bytes 49160 | tf_op jit(solution)/shard_map/ppermute | solution.py:30
  400.8 9.5 %collective-permute-start.15 = (f32[2,2,1,1,1024]{4,3,0,2,1:T(1,128)S(1)}, f32[2,2,1,1,1024]{4,3,0,2,1:T(1,128)S(1)}, u32[]{:S(2)}, u32[]{:S(2)}) collective-permute-start(f32[2,2,1,1,1024]{4,3,0,2,1:T(1,128)S(1)} %get-tuple-element.49), channel_id=1, source_target_pairs={{0,1},{1,2},{2,3},{3,4},{4,5},{5,6},{6,7},{7,8},{8,9},{9,10},{10,1... | collective-permute-start | bytes 49160 | tf_op jit(solution)/shard_map/ppermute | solution.py:27
  409.0 8.4 %collective-permute-start.14 = (f32[2,2,1,1,1024]{4,3,0,2,1:T(1,128)S(1)}, f32[2,2,1,1,1024]{4,3,0,2,1:T(1,128)S(1)}, u32[]{:S(2)}, u32[]{:S(2)}) collective-permute-start(f32[2,2,1,1,1024]{4,3,0,2,1:T(1,128)S(1)} %get-tuple-element.48), channel_id=1, source_target_pairs={{1,0},{2,1},{3,2},{4,3},{5,4},{6,5},{7,6},{8,7},{9,8},{10,9},{11,1... | collective-permute-start | bytes 49160 | tf_op jit(solution)/shard_map/ppermute | solution.py:30
  417.7 14.0 %copy-start = (f32[16,1024]{1,0:T(8,128)S(1)}, f32[16,1024]{1,0:T(8,128)}, u32[]{:S(2)}) copy-start(f32[16,1024]{1,0:T(8,128)} %get-tuple-element.9) | copy-start | bytes 196612
  417.7 6.6 %collective-permute-start.17 = (f32[2,2,1,1,1024]{4,3,0,2,1:T(1,128)S(1)}, f32[2,2,1,1,1024]{4,3,0,2,1:T(1,128)S(1)}, u32[]{:S(2)}, u32[]{:S(2)}) collective-permute-start(f32[2,2,1,1,1024]{4,3,0,2,1:T(1,128)S(1)} %get-tuple-element.47), channel_id=1, source_target_pairs={{0,1},{1,2},{2,3},{3,4},{4,5},{5,6},{6,7},{7,8},{8,9},{9,10},{10,1... | collective-permute-start | bytes 49160 | tf_op jit(solution)/shard_map/ppermute | solution.py:27
  422.9 8.4 %collective-permute-start.16 = (f32[2,2,1,1,1024]{4,3,0,2,1:T(1,128)S(1)}, f32[2,2,1,1,1024]{4,3,0,2,1:T(1,128)S(1)}, u32[]{:S(2)}, u32[]{:S(2)}) collective-permute-start(f32[2,2,1,1,1024]{4,3,0,2,1:T(1,128)S(1)} %get-tuple-element.46), channel_id=1, source_target_pairs={{1,0},{2,1},{3,2},{4,3},{5,4},{6,5},{7,6},{8,7},{9,8},{10,9},{11,1... | collective-permute-start | bytes 49160 | tf_op jit(solution)/shard_map/ppermute | solution.py:30
  432.1 6.3 collective-permute-start.19
  437.0 8.4 %collective-permute-start.18 = (f32[2,2,1,1,1024]{4,3,0,2,1:T(1,128)S(1)}, f32[2,2,1,1,1024]{4,3,0,2,1:T(1,128)S(1)}, u32[]{:S(2)}, u32[]{:S(2)}) collective-permute-start(f32[2,2,1,1,1024]{4,3,0,2,1:T(1,128)S(1)} %get-tuple-element.44), channel_id=1, source_target_pairs={{1,0},{2,1},{3,2},{4,3},{5,4},{6,5},{7,6},{8,7},{9,8},{10,9},{11,1... | collective-permute-start | bytes 49160 | tf_op jit(solution)/shard_map/ppermute | solution.py:30
  445.7 6.5 %collective-permute-start.21 = (f32[2,2,1,1,1024]{4,3,0,2,1:T(1,128)S(1)}, f32[2,2,1,1,1024]{4,3,0,2,1:T(1,128)S(1)}, u32[]{:S(2)}, u32[]{:S(2)}) collective-permute-start(f32[2,2,1,1,1024]{4,3,0,2,1:T(1,128)S(1)} %get-tuple-element.43), channel_id=1, source_target_pairs={{0,1},{1,2},{2,3},{3,4},{4,5},{5,6},{6,7},{7,8},{8,9},{9,10},{10,1... | collective-permute-start | bytes 49160 | tf_op jit(solution)/shard_map/ppermute | solution.py:27
  450.8 8.4 %collective-permute-start.20 = (f32[2,2,1,1,1024]{4,3,0,2,1:T(1,128)S(1)}, f32[2,2,1,1,1024]{4,3,0,2,1:T(1,128)S(1)}, u32[]{:S(2)}, u32[]{:S(2)}) collective-permute-start(f32[2,2,1,1,1024]{4,3,0,2,1:T(1,128)S(1)} %get-tuple-element.42), channel_id=1, source_target_pairs={{1,0},{2,1},{3,2},{4,3},{5,4},{6,5},{7,6},{8,7},{9,8},{10,9},{11,1... | collective-permute-start | bytes 49160 | tf_op jit(solution)/shard_map/ppermute | solution.py:30
  459.5 6.9 %collective-permute-start.23 = (f32[2,2,1,1,1024]{4,3,0,2,1:T(1,128)S(1)}, f32[2,2,1,1,1024]{4,3,0,2,1:T(1,128)S(1)}, u32[]{:S(2)}, u32[]{:S(2)}) collective-permute-start(f32[2,2,1,1,1024]{4,3,0,2,1:T(1,128)S(1)} %get-tuple-element.41), channel_id=1, source_target_pairs={{0,1},{1,2},{2,3},{3,4},{4,5},{5,6},{6,7},{7,8},{8,9},{9,10},{10,1... | collective-permute-start | bytes 49160 | tf_op jit(solution)/shard_map/ppermute | solution.py:27
  465.1 8.4 %collective-permute-start.22 = (f32[2,2,1,1,1024]{4,3,0,2,1:T(1,128)S(1)}, f32[2,2,1,1,1024]{4,3,0,2,1:T(1,128)S(1)}, u32[]{:S(2)}, u32[]{:S(2)}) collective-permute-start(f32[2,2,1,1,1024]{4,3,0,2,1:T(1,128)S(1)} %get-tuple-element.40), channel_id=1, source_target_pairs={{1,0},{2,1},{3,2},{4,3},{5,4},{6,5},{7,6},{8,7},{9,8},{10,9},{11,1... | collective-permute-start | bytes 49160 | tf_op jit(solution)/shard_map/ppermute | solution.py:30
  474.8 1.7 copy-start.3
  629.9 9.5 %collective-permute-start.24 = (f32[5,16,1]{2,1,0:T(8,128)S(1)}, f32[5,16,1]{2,1,0:T(8,128)S(1)}, u32[]{:S(2)}, u32[]{:S(2)}) collective-permute-start(f32[5,16,1]{2,1,0:T(8,128)S(1)} %get-tuple-element.95), channel_id=1, source_target_pairs={{0,16},{16,32},{32,48},{48,64},{64,80},{80,96},{96,112},{112,128},... | collective-permute-start | bytes 968 | tf_op jit(solution)/shard_map/ppermute | solution.py:27
  632.7 6.7 %collective-permute-start.25 = (f32[5,16,1]{2,1,0:T(8,128)S(1)}, f32[5,16,1]{2,1,0:T(8,128)S(1)}, u32[]{:S(2)}, u32[]{:S(2)}) collective-permute-start(f32[5,16,1]{2,1,0:T(8,128)S(1)} %get-tuple-element.94), channel_id=1, source_target_pairs={{16,0},{32,16},{48,32},{64,48},{80,64},{96,80},{112,96},{128,112},... | collective-permute-start | bytes 968 | tf_op jit(solution)/shard_map/ppermute | solution.py:30
Sparse Core Ops, SparseCore 0:
  12.9 286.4 all-reduce.14
  476.6 152.2 reduce-scatter.3
where the time goes:
time: 648 us; the launch traced here: 647 us
  waiting for transfers between devices  524 us (81%)
  starting transfers between devices  91.6 us (14%)
  between operations  17.4 us (3%)
  other arithmetic  8.81 us (1%)
    psum x1, waiting for transfers between devices, from_root(): return lax.psum(block, axis)  287 us
    unnamed x3, waiting for transfers between devices  152 us
    ppermute x13, waiting for transfers between devices, extended(): lax.ppermute(lax.slice_in_dim(block, 0, width, axis=dim), axis, backward)  84.7 us
    ppermute x13, starting transfers between devices, extended(): lax.ppermute(lax.slice_in_dim(block, block.shape[dim] - width, None, axis...  70.1 us
    ppermute x13, starting transfers between devices, extended(): lax.ppermute(lax.slice_in_dim(block, 0, width, axis=dim), axis, backward)  21.4 us
  transfers between devices with their start and end apart: 28, of which 15 were waited for; matrix products, arithmetic and copies ran while one was open for 0% of the time, Pallas kernels for 0%

commit v1 on v0

v1 whole, which is shorter than its diff:
```python
import functools
import math

import jax
import jax.numpy as jnp
from jax import lax
from jax.experimental import pallas as pl
from jax.experimental.pallas import tpu as pltpu
from jax.sharding import PartitionSpec as P

MESH = pl.DeviceIdType.MESH
DEPTHS = 4
SWEEPS = 3
HALO = DEPTHS * SWEEPS
ROWS = 16
DAMPING = 0.125
ROTATION = 0.125
STEP_DEPTH = 4.0
SMOOTHING = 0.25


def remote(src, dst, send, recv, device):
    return pltpu.make_async_remote_copy(
        src_ref=src,
        dst_ref=dst,
        send_sem=send,
        recv_sem=recv,
        device_id=device,
        device_id_type=MESH,
    )


def sin_cos(theta):
    turns = jnp.floor(theta * (2.0 / math.pi) + 0.5)
    rest = theta - turns * 1.5703125
    rest = rest - turns * 4.837512969970703125e-4
    rest = rest - turns * 7.54978995489188216e-8
    sq = rest * rest
    sine = ((-1.9515295891e-4 * sq + 8.3321608736e-3) * sq - 1.6666654611e-1) * sq * rest + rest
    cosine = (
        ((2.443315711809948e-5 * sq - 1.388731625493765e-3) * sq + 4.166664568298827e-2) * sq * sq
        - 0.5 * sq
        + 1.0
    )
    odd = turns - 2.0 * jnp.floor(turns * 0.5)
    back = turns - 4.0 * jnp.floor(turns * 0.25) - odd
    sign = 1.0 - back
    sin_val = jnp.where(odd > 0.5, cosine, sine) * sign
    cos_val = jnp.where(odd > 0.5, -sine, cosine) * sign
    return sin_val, cos_val


def kernel(
    freqs, tiles,
    src, rcv, vel, own, reg,
    wave_out, img_out,
    raw, velraw, regbuf, ownbuf, buf_a, buf_b, vels, stage, recv, labs, weights, imgb, pack, parts, wave, img,
    local_sem, first_sem, field_sem, vhalo_sem, z_sem, x_sem, core_sem, image_sem,
):
    f = lax.axis_index("freq")
    t = lax.axis_index("tile")
    after = lax.rem(t + 1, tiles)
    before = lax.rem(t + tiles - 1, tiles)
    core = lax.rem(f, 2)
    row = f // 2
    xx = row // 4
    zz = lax.rem(row, 4)

    barrier = pltpu.get_barrier_semaphore()

    def signal(i, carry):
        pl.semaphore_signal(
            barrier, inc=1, device_id=(lax.rem(f + i, freqs), t), device_id_type=MESH
        )
        return carry

    for tile in (after, before):
        pl.semaphore_signal(barrier, inc=1, device_id=(f, tile), device_id_type=MESH)
    lax.fori_loop(1, freqs, signal, 0)

    loads = [
        pltpu.make_async_copy(vel, velraw, local_sem.at[0]),
        pltpu.make_async_copy(reg, regbuf, local_sem.at[1]),
        pltpu.make_async_copy(own, ownbuf, local_sem.at[2]),
        pltpu.make_async_copy(src, raw.at[pl.ds(0, 2)], local_sem.at[3]),
        pltpu.make_async_copy(rcv, raw.at[pl.ds(2, 2)], local_sem.at[4]),
    ]
    for copy in loads:
        copy.start()

    loads[0].wait()
    for half in range(2):
        for c in range(8):
            stage[pl.ds(128 * half + 8 * (c // 4) + c % 4, 8, stride=16), :] = velraw[
                8 * half : 8 * half + 8, 128 * c : 128 * c + 128
            ]
    loads[1].wait()
    own_labels = regbuf[...].astype(jnp.float32) + 1.0
    own_labels = jnp.concatenate([own_labels[4 * m : 4 * m + 4] for m in range(4)], axis=1)
    for j in range(32):
        stage[8 * j + 4 : 8 * j + 8, :] = own_labels
    mine = pl.ds(pl.multiple_of(8 * f, 8), 8)
    recv[mine, :] = stage[mine, :]
    loads[3].wait()
    loads[4].wait()
    for a in range(4):
        for half in range(2):
            for c in range(8):
                buf_a[a, pl.ds(8 * (16 + 8 * half) + c, 8, stride=8), :] = raw[
                    a, 8 * half : 8 * half + 8, 128 * c : 128 * c + 128
                ]
    loads[2].wait()

    pl.semaphore_wait(barrier, freqs + 1)

    def first_send(i, carry):
        d = lax.rem(f + i, freqs)
        remote(
            stage.at[pl.ds(pl.multiple_of(8 * d, 8), 8)],
            recv.at[mine],
            first_sem.at[0],
            first_sem.at[1],
            (d, t),
        ).start()
        return carry

    lax.fori_loop(1, freqs, first_send, 0)
    fields = []
    for a in range(4):
        for k, (lo, to, tile) in enumerate(((20, 4, after), (16, 32, before))):
            fields.append(
                remote(
                    buf_a.at[a, pl.ds(8 * lo, 8 * HALO)],
                    buf_a.at[a, pl.ds(8 * to, 8 * HALO)],
                    field_sem.at[0, 2 * a + k],
                    field_sem.at[1, 2 * a + k],
                    (f, tile),
                )
            )
    for copy in fields:
        copy.start()

    bulk = pl.ds(0, 8 * (freqs - 1))
    first_wait = remote(stage.at[bulk], recv.at[bulk], first_sem.at[0], first_sem.at[1], (f, after))
    first_wait.wait_recv()
    wanted = [jnp.full((8, 128), ownbuf[d], jnp.int32) for d in range(DEPTHS)]
    picked = [jnp.ones((8, 128), jnp.float32)] * DEPTHS
    for j in range(32):
        piece = recv[8 * j : 8 * j + 8, :]
        picked = [jnp.where(w == j, piece, p) for w, p in zip(wanted, picked)]
    for c in range(2):

        @pl.when(core == c)
        def _():
            for d in range(DEPTHS):
                vels[d, 16 + row, 4 * c : 4 * c + 4, :] = picked[d][0:4]

    lanes = pl.ds(pl.multiple_of(4 * core, 4), 4)

    def block(part, first, count):
        return vels.at[:, pl.ds(16 * part + first, count), lanes]

    z_peers = [((xx * 4 + lax.rem(zz + i, 4)) * 2 + core, t) for i in (1, 2, 3)]
    x_peers = [((lax.rem(xx + i, 4) * 4 + zz) * 2 + core, t) for i in (1, 2, 3)]
    core_peer = (row * 2 + 1 - core, t)

    def spread(part, first, count, sems, peers):
        piece = block(part, first, count)
        copies = [
            remote(piece, piece, sems.at[0, part, i], sems.at[1, part, i], peer)
            for i, peer in enumerate(peers)
        ]
        for copy in copies:
            copy.start()
        return copies

    vhalos = [
        remote(block(1, row, 1), block(0, row, 1), vhalo_sem.at[0, 0], vhalo_sem.at[1, 0], (f, after)),
        remote(block(1, row, 1), block(2, row, 1), vhalo_sem.at[0, 1], vhalo_sem.at[1, 1], (f, before)),
    ]
    for copy in vhalos:
        copy.start()
    z_own = spread(1, row, 1, z_sem, z_peers)

    lane = lax.broadcasted_iota(jnp.int32, (8, 128), 1)
    sub = lax.broadcasted_iota(jnp.int32, (8, 128), 0)
    first_lane, last_lane = lane == 0, lane == 127
    start_cell = first_lane & (sub == 0)
    end_cell = last_lane & (sub == 7)
    group = [(lane >= 32 * m) & (lane < 32 * m + 32) for m in range(4)]

    def shifted(ref, at, middle):
        up = jnp.where(first_lane, ref[pl.ds(at + 1, 8), :], middle)
        down = jnp.where(last_lane, ref[pl.ds(at - 1, 8), :], middle)
        return pltpu.roll(up, 127, 1), pltpu.roll(down, 1, 1)

    for i in range(4):
        cols = [recv[pl.ds(8 * q + 4 + i, 8, stride=32), :] for q in range(4)]
        for m in range(4):
            total = None
            for q in range(4):
                moved = cols[q] if q == m else pltpu.roll(cols[q], (32 * (q - m)) % 128, 1)
                total = moved if total is None else jnp.where(group[q], moved, total)
            labs[8 * (4 * m + i + 1) : 8 * (4 * m + i + 2), :] = total
    scale = SMOOTHING / math.sqrt(freqs)
    for r in range(ROWS):
        middle = labs[8 * (r + 1) : 8 * (r + 2), :]
        up, down = shifted(labs, 8 * (r + 1), middle)
        weights[0, 8 * r : 8 * r + 8, :] = jnp.where((up == middle) & ~end_cell, scale, 0.0)
        weights[1, 8 * r : 8 * r + 8, :] = jnp.where((down == middle) & ~start_cell, scale, 0.0)

    for copy in z_own:
        copy.wait_recv()
    x_own = spread(1, 4 * xx, 4, x_sem, x_peers)
    for copy in vhalos:
        copy.wait_recv()
    z_halo = [spread(part, row, 1, z_sem, z_peers) for part in (0, 2)]
    for copy in x_own:
        copy.wait_recv()
    c_own = spread(1, 0, 16, core_sem, [core_peer])
    for copy in z_halo[0] + z_halo[1]:
        copy.wait_recv()
    x_halo = [spread(part, 4 * xx, 4, x_sem, x_peers) for part in (0, 2)]
    for copy in x_halo[0] + x_halo[1]:
        copy.wait_recv()
    c_halo = [spread(part, 0, 16, core_sem, [core_peer]) for part in (0, 2)]
    for copy in c_own + c_halo[0] + c_halo[1]:
        copy.wait_recv()
    for copy in fields:
        copy.wait()

    omega = 1.0 + f.astype(jnp.float32) / freqs
    reach = omega * STEP_DEPTH
    turn = ROTATION / omega

    def close(ref):
        zero = jnp.zeros((8, 128), jnp.float32)
        for edge, at in ((0, 15), (tiles - 1, 32)):

            @pl.when(t == edge)
            def _():
                for a in range(4):
                    ref[a, 8 * at : 8 * at + 8, :] = zero

    def rotate(ref, d, i):
        at = pl.ds(pl.multiple_of(8 * i, 8), 8)
        sine, cosine = sin_cos(reach / vels[d, i])
        s0, s1, r0, r1 = (ref[a, at, :] for a in range(4))
        ref[0, at, :] = s0 * cosine - s1 * sine
        ref[1, at, :] = s0 * sine + s1 * cosine
        ref[2, at, :] = r0 * cosine + r1 * sine
        ref[3, at, :] = r1 * cosine - r0 * sine

    def sweep(old, new, d, i):
        base = pl.multiple_of(8 * i, 8)
        coeff = vels[d, i] * turn
        middles, spreads = [], []
        for a in range(4):
            ref = old.at[a]
            middle = ref[pl.ds(base, 8), :]
            up, down = shifted(ref, base, middle)
            beside_y = jnp.where(end_cell, 0.0, up) + jnp.where(start_cell, 0.0, down)
            beside_x = ref[pl.ds(base + 8, 8), :] + ref[pl.ds(base - 8, 8), :]
            middles.append(middle)
            spreads.append(beside_x + beside_y - 4.0 * middle)
        for k, sign in ((0, 1.0), (2, -1.0)):
            signed = coeff * sign
            new[k, pl.ds(base, 8), :] = (
                middles[k] + DAMPING * spreads[k] - signed * spreads[k + 1]
            )
            new[k + 1, pl.ds(base, 8), :] = (
                middles[k + 1] + DAMPING * spreads[k + 1] + signed * spreads[k]
            )

    def over_rows(low, high, width, body):
        steps = (high - low) // width

        def go(n, carry):
            for k in range(width):
                body(low + width * n + k)
            return carry

        lax.fori_loop(0, steps, go, 0)
        for i in range(low + steps * width, high):
            body(i)

    close(buf_a)
    now, later = buf_a, buf_b
    bulk_pack = pl.ds(0, 4 * (freqs - 1))
    for d in range(DEPTHS):
        low = 4 + SWEEPS * d
        over_rows(low, 48 - low, 4, functools.partial(rotate, now, d))
        for s in range(SWEEPS):
            low += 1
            over_rows(low, 48 - low, 8, functools.partial(sweep, now, later, d))
            close(later)
            now, later = later, now

        for r in range(ROWS):
            at = slice(8 * (16 + r), 8 * (17 + r))
            imgb[8 * (r + 1) : 8 * (r + 2), :] = (
                now[0, at, :] * now[2, at, :] + now[1, at, :] * now[3, at, :]
            )
        smooth = []
        for r in range(ROWS):
            middle = imgb[8 * (r + 1) : 8 * (r + 2), :]
            up, down = shifted(imgb, 8 * (r + 1), middle)
            nxt, prv = weights[0, 8 * r : 8 * r + 8, :], weights[1, 8 * r : 8 * r + 8, :]
            smooth.append(
                middle * (1.0 / math.sqrt(freqs))
                + nxt * (jnp.where(end_cell, 0.0, up) - middle)
                + prv * (jnp.where(start_cell, 0.0, down) - middle)
            )
        for q in range(4):
            for i in range(4):
                total = None
                for m in range(4):
                    line = smooth[4 * m + i]
                    moved = line if m == q else pltpu.roll(line, (32 * (m - q)) % 128, 1)
                    total = moved if total is None else jnp.where(group[m], moved, total)
                pack[d, pl.ds(4 * q + i, 8, stride=16), :] = total
        own_piece = pl.ds(pl.multiple_of(4 * f, 4), 4)
        parts[d, own_piece, :] = pack[d, own_piece, :]

        def image_send(i, carry):
            to = lax.rem(f + i, freqs)
            remote(
                pack.at[d, pl.ds(pl.multiple_of(4 * to, 4), 4)],
                parts.at[d, own_piece],
                image_sem.at[0, d],
                image_sem.at[1, d],
                (to, t),
            ).start()
            return carry

        lax.fori_loop(1, freqs, image_send, 0)

    for a in range(4):
        for half in range(2):
            for c in range(8):
                wave[a, 8 * half : 8 * half + 8, 128 * c : 128 * c + 128] = now[
                    a, pl.ds(8 * (16 + 8 * half) + c, 8, stride=8), :
                ]
    wave_copy = pltpu.make_async_copy(wave, wave_out, local_sem.at[0])
    wave_copy.start()

    first_wait.wait_send()
    for copy in vhalos + z_own + x_own + c_own:
        copy.wait_send()
    for group_of in (z_halo, x_halo, c_halo):
        for copy in group_of[0] + group_of[1]:
            copy.wait_send()

    for d in range(DEPTHS):
        done = remote(
            pack.at[d, bulk_pack], parts.at[d, bulk_pack], image_sem.at[0, d], image_sem.at[1, d], (f, after)
        )
        done.wait_recv()
        total = parts[d, 0:8, :]
        for j in range(1, 16):
            total = total + parts[d, 8 * j : 8 * j + 8, :]
        total = total[0:4] + total[4:8]
        for m in range(4):
            img[d, 4 * m : 4 * m + 4, :] = total[:, 32 * m : 32 * m + 32]
        done.wait_send()
    img_copy = pltpu.make_async_copy(img, img_out, local_sem.at[1])
    img_copy.start()
    wave_copy.wait()
    img_copy.wait()


def solution(mesh):
    freqs, tiles = mesh.shape["freq"], mesh.shape["tile"]

    def on_device(source_field, receiver_field, velocity_store, slice_owner, region_map):
        any_space = pl.BlockSpec(memory_space=pl.ANY)
        f32 = jnp.float32
        wave, image = pl.pallas_call(
            functools.partial(kernel, freqs, tiles),
            out_shape=[
                jax.ShapeDtypeStruct((4, 16, 1024), f32),
                jax.ShapeDtypeStruct((DEPTHS, 16, 32), f32),
            ],
            in_specs=[any_space] * 5,
            out_specs=[any_space] * 2,
            scratch_shapes=[
                pltpu.VMEM((4, 16, 1024), f32),
                pltpu.VMEM((16, 1024), f32),
                pltpu.VMEM((16, 32), jnp.int32),
                pltpu.SMEM((DEPTHS,), jnp.int32),
                pltpu.VMEM((4, 48 * 8, 128), f32),
                pltpu.VMEM((4, 48 * 8, 128), f32),
                pltpu.VMEM((DEPTHS, 48, 8, 128), f32),
                pltpu.VMEM((32 * 8, 128), f32),
                pltpu.VMEM((32 * 8, 128), f32),
                pltpu.VMEM((18 * 8, 128), f32),
                pltpu.VMEM((2, 16 * 8, 128), f32),
                pltpu.VMEM((18 * 8, 128), f32),
                pltpu.VMEM((DEPTHS, 32 * 4, 128), f32),
                pltpu.VMEM((DEPTHS, 32 * 4, 128), f32),
                pltpu.VMEM((4, 16, 1024), f32),
                pltpu.VMEM((DEPTHS, 16, 32), f32),
                pltpu.SemaphoreType.DMA((5,)),
                pltpu.SemaphoreType.DMA((2,)),
                pltpu.SemaphoreType.DMA((2, 8)),
                pltpu.SemaphoreType.DMA((2, 2)),
                pltpu.SemaphoreType.DMA((2, 3, 3)),
                pltpu.SemaphoreType.DMA((2, 3, 3)),
                pltpu.SemaphoreType.DMA((2, 3, 1)),
                pltpu.SemaphoreType.DMA((2, DEPTHS)),
            ],
            compiler_params=pltpu.CompilerParams(
                collective_id=0, has_side_effects=True, vmem_limit_bytes=60 * 1024 * 1024
            ),
        )(
            source_field[:, 0],
            receiver_field[:, 0],
            velocity_store[0],
            slice_owner,
            region_map,
        )
        return wave.reshape(2, 2, 1, 16, 1024), image

    in_specs = (
        P(None, "freq", "tile", None),
        P(None, "freq", "tile", None),
        P("freq", "tile", None),
        P(),
        P("tile", "freq"),
    )
    out_specs = (P(None, None, "freq", "tile", None), P(None, "tile", "freq"))
    return jax.shard_map(
        on_device, mesh=mesh, in_specs=in_specs, out_specs=out_specs, check_vma=False
    )
```

time: 648 us -> 72.1 us (0.11)
  waiting for transfers between devices: 524 us -> 0 us
  starting transfers between devices: 91.6 us -> 0 us
  Pallas kernels: 0 us -> 69 us
  between operations: 17.4 us -> 0.65 us
  other arithmetic: 8.81 us -> 0 us
    psum x1 -> x0, waiting for transfers between devices: 287 us -> none  [from_root(): return lax.psum(block, axis)]
    unnamed x3 -> x0, waiting for transfers between devices: 152 us -> none
    ppermute x26 -> x0, starting transfers between devices: 91.5 us -> none  [the longest x13 70.1 us: extended(): lax.ppermute(lax.slice_in_dim(block, block.shape[dim] - width, None, axis...]
    ppermute x26 -> x0, waiting for transfers between devices: 84.8 us -> none  [the longest x13 84.7 us: extended(): lax.ppermute(lax.slice_in_dim(block, 0, width, axis=dim), axis, backward)]
    pallas_call x0 -> x1, Pallas kernels: none -> 69 us  [on_device(): pl.pallas_call(functools.partial(kernel, freqs, tiles), out_shape=[jax.Sh...]
  transfers between devices with their start and end apart: 28 -> 0, of which waited for: 15 -> 0; matrix products, arithmetic and copies ran while one was open for 0% -> 0% of each run, Pallas kernels for 0% -> 0%
where the time goes in v1:
time: 72.1 us; the launch traced here: 72 us
  Pallas kernels  69 us (96%)
  local copies, waits for them, and re-layouts  2.3 us (3%)
    pallas_call x1, Pallas kernels, on_device(): pl.pallas_call(functools.partial(kernel, freqs, tiles), out_shape=[jax.Sh...  69 us
    unnamed x4, local copies, waits for them, and re-layouts  2.3 us

profile of v1, /device:TPU:1, one launch (start us, length us, event | category | flops | bytes accessed | tf_op | source)
XLA Modules:
  0.0 72.0 jit_solution(12993253099714680560)
XLA Ops:
  0.6 69.0 %shard_map.68 = (f32[4,16,1024]{2,1,0:T(8,128)}, f32[4,16,32]{2,1,0:T(8,128)}) custom-call(f32[2,16,1024]{2,1,0:T(8,128)} %bitcast.7, f32[2,16,1024]{2,1,0:T(8,128)} %bitcast.8, f32[16,1024]{1,0:T(8,128)} %bitcast.9, s32[4]{0:T(128)} %own.1, s32[16,32]{1,0:T(8,128)} %reg.1), custom_call_target="tpu_custom_call" | custom-call | tf_op jit(solution)/shard_map/pallas_call | solution.py:378
  69.7 0.0 copy-start
  69.7 1.7 %copy.10 = f32[2,2,1,16,1024]{4,3,2,1,0:T(8,128)} copy(f32[2,2,1,16,1024]{4,3,2,1,0:T(8,128)} %bitcast.6) | data formatting | bytes 524288
  71.3 0.0 copy-done
  71.3 0.6 copy.11
Async XLA Ops:
  69.7 1.7 %copy-start = (f32[4,16,32]{2,1,0:T(8,128)S(1)}, f32[4,16,32]{2,1,0:T(8,128)}, u32[]{:S(2)}) copy-start(f32[4,16,32]{2,1,0:T(8,128)} %get-tuple-element.11) | copy-start | bytes 24580

commit v2 on v1

--- a/solution.py
+++ b/solution.py
@@ -13,6 +13,7 @@
 SWEEPS = 3
 HALO = DEPTHS * SWEEPS
 ROWS = 16
+CHUNKS = ((0, 3), (3, 6), (6, 8), (8, 12))
 DAMPING = 0.125
 ROTATION = 0.125
 STEP_DEPTH = 4.0
@@ -126,19 +127,25 @@
 
     lax.fori_loop(1, freqs, first_send, 0)
     fields = []
-    for a in range(4):
-        for k, (lo, to, tile) in enumerate(((20, 4, after), (16, 32, before))):
-            fields.append(
-                remote(
-                    buf_a.at[a, pl.ds(8 * lo, 8 * HALO)],
-                    buf_a.at[a, pl.ds(8 * to, 8 * HALO)],
-                    field_sem.at[0, 2 * a + k],
-                    field_sem.at[1, 2 * a + k],
+
+    def send_fields(chunk):
+        near, far = CHUNKS[chunk]
+        count = 8 * (far - near)
+        for a in range(4):
+            for k, (lo, to, tile) in enumerate(
+                ((32 - far, 16 - far, after), (16 + near, 32 + near, before))
+            ):
+                copy = remote(
+                    buf_a.at[a, pl.ds(8 * lo, count)],
+                    buf_a.at[a, pl.ds(8 * to, count)],
+                    field_sem.at[0, chunk, 2 * a + k],
+                    field_sem.at[1, chunk, 2 * a + k],
                     (f, tile),
                 )
-            )
-    for copy in fields:
-        copy.start()
+                copy.start()
+                fields.append(copy)
+
+    send_fields(0)
 
     bulk = pl.ds(0, 8 * (freqs - 1))
     first_wait = remote(stage.at[bulk], recv.at[bulk], first_sem.at[0], first_sem.at[1], (f, after))
@@ -181,6 +188,7 @@
     for copy in vhalos:
         copy.start()
     z_own = spread(1, row, 1, z_sem, z_peers)
+    send_fields(1)
 
     lane = lax.broadcasted_iota(jnp.int32, (8, 128), 1)
     sub = lax.broadcasted_iota(jnp.int32, (8, 128), 0)
@@ -215,12 +223,14 @@
     for copy in vhalos:
         copy.wait_recv()
     z_halo = [spread(part, row, 1, z_sem, z_peers) for part in (0, 2)]
+    send_fields(2)
     for copy in x_own:
         copy.wait_recv()
     c_own = spread(1, 0, 16, core_sem, [core_peer])
     for copy in z_halo[0] + z_halo[1]:
         copy.wait_recv()
     x_halo = [spread(part, 4 * xx, 4, x_sem, x_peers) for part in (0, 2)]
+    send_fields(3)
     for copy in x_halo[0] + x_halo[1]:
         copy.wait_recv()
     c_halo = [spread(part, 0, 16, core_sem, [core_peer]) for part in (0, 2)]
@@ -289,10 +299,10 @@
     bulk_pack = pl.ds(0, 4 * (freqs - 1))
     for d in range(DEPTHS):
         low = 4 + SWEEPS * d
-        over_rows(low, 48 - low, 4, functools.partial(rotate, now, d))
+        over_rows(low, 48 - low, (48 - 2 * low) // 2, functools.partial(rotate, now, d))
         for s in range(SWEEPS):
             low += 1
-            over_rows(low, 48 - low, 8, functools.partial(sweep, now, later, d))
+            over_rows(low, 48 - low, (48 - 2 * low) // 2, functools.partial(sweep, now, later, d))
             close(later)
             now, later = later, now
 
@@ -402,7 +412,7 @@
                 pltpu.VMEM((DEPTHS, 16, 32), f32),
                 pltpu.SemaphoreType.DMA((5,)),
                 pltpu.SemaphoreType.DMA((2,)),
-                pltpu.SemaphoreType.DMA((2, 8)),
+                pltpu.SemaphoreType.DMA((2, len(CHUNKS), 8)),
                 pltpu.SemaphoreType.DMA((2, 2)),
                 pltpu.SemaphoreType.DMA((2, 3, 3)),
                 pltpu.SemaphoreType.DMA((2, 3, 3)),

time: 72.1 us -> 62.8 us (0.87)
  Pallas kernels: 69 us -> 59.4 us
    pallas_call x1, Pallas kernels: 69 us -> 59.4 us  [on_device(): pl.pallas_call(functools.partial(kernel, freqs, tiles), out_shape=[jax.Sh...]
where the time goes in v2:
time: 62.8 us; the launch traced here: 62.4 us
  Pallas kernels  59.4 us (95%)
  local copies, waits for them, and re-layouts  2.3 us (4%)
  between operations  0.65 us (1%)
    pallas_call x1, Pallas kernels, on_device(): pl.pallas_call(functools.partial(kernel, freqs, tiles), out_shape=[jax.Sh...  59.4 us
    unnamed x4, local copies, waits for them, and re-layouts  2.3 us

profile of v2, /device:TPU:1, one launch (start us, length us, event | category | flops | bytes accessed | tf_op | source)
XLA Modules:
  0.0 62.4 jit_solution(220792911555907156)
XLA Ops:
  0.6 59.4 %shard_map.68 = (f32[4,16,1024]{2,1,0:T(8,128)}, f32[4,16,32]{2,1,0:T(8,128)}) custom-call(f32[2,16,1024]{2,1,0:T(8,128)} %bitcast.7, f32[2,16,1024]{2,1,0:T(8,128)} %bitcast.8, f32[16,1024]{1,0:T(8,128)} %bitcast.9, s32[4]{0:T(128)} %own.1, s32[16,32]{1,0:T(8,128)} %reg.1), custom_call_target="tpu_custom_call" | custom-call | tf_op jit(solution)/shard_map/pallas_call | solution.py:388
  60.1 0.0 copy-start
  60.1 1.7 %copy.10 = f32[2,2,1,16,1024]{4,3,2,1,0:T(8,128)} copy(f32[2,2,1,16,1024]{4,3,2,1,0:T(8,128)} %bitcast.6) | data formatting | bytes 524288
  61.7 0.0 copy-done
  61.7 0.6 copy.11
Async XLA Ops:
  60.1 1.7 %copy-start = (f32[4,16,32]{2,1,0:T(8,128)S(1)}, f32[4,16,32]{2,1,0:T(8,128)}, u32[]{:S(2)}) copy-start(f32[4,16,32]{2,1,0:T(8,128)} %get-tuple-element.11) | copy-start | bytes 24580

commit v3 on v2

--- a/solution.py
+++ b/solution.py
@@ -13,7 +13,7 @@
 SWEEPS = 3
 HALO = DEPTHS * SWEEPS
 ROWS = 16
-CHUNKS = ((0, 3), (3, 6), (6, 8), (8, 12))
+CHUNKS = ((0, 3), (3, 6), (6, 7), (7, 12))
 DAMPING = 0.125
 ROTATION = 0.125
 STEP_DEPTH = 4.0
@@ -54,8 +54,8 @@
 def kernel(
     freqs, tiles,
     src, rcv, vel, own, reg,
-    wave_out, img_out,
-    raw, velraw, regbuf, ownbuf, buf_a, buf_b, vels, stage, recv, labs, weights, imgb, pack, parts, wave, img,
+    wave, img,
+    raw, velraw, regbuf, ownbuf, buf_a, buf_b, vels, stage, recv, labs, weights, imgb, pack, parts,
     local_sem, first_sem, field_sem, vhalo_sem, z_sem, x_sem, core_sem, image_sem,
 ):
     f = lax.axis_index("freq")
@@ -67,18 +67,6 @@
     xx = row // 4
     zz = lax.rem(row, 4)
 
-    barrier = pltpu.get_barrier_semaphore()
-
-    def signal(i, carry):
-        pl.semaphore_signal(
-            barrier, inc=1, device_id=(lax.rem(f + i, freqs), t), device_id_type=MESH
-        )
-        return carry
-
-    for tile in (after, before):
-        pl.semaphore_signal(barrier, inc=1, device_id=(f, tile), device_id_type=MESH)
-    lax.fori_loop(1, freqs, signal, 0)
-
     loads = [
         pltpu.make_async_copy(vel, velraw, local_sem.at[0]),
         pltpu.make_async_copy(reg, regbuf, local_sem.at[1]),
@@ -88,6 +76,18 @@
     ]
     for copy in loads:
         copy.start()
+
+    barrier = pltpu.get_barrier_semaphore()
+
+    def signal(i, carry):
+        pl.semaphore_signal(
+            barrier, inc=1, device_id=(lax.rem(f + i, freqs), t), device_id_type=MESH
+        )
+        return carry
+
+    for tile in (after, before):
+        pl.semaphore_signal(barrier, inc=1, device_id=(f, tile), device_id_type=MESH)
+    lax.fori_loop(1, freqs, signal, 0)
 
     loads[0].wait()
     for half in range(2):
@@ -302,7 +302,7 @@
         over_rows(low, 48 - low, (48 - 2 * low) // 2, functools.partial(rotate, now, d))
         for s in range(SWEEPS):
             low += 1
-            over_rows(low, 48 - low, (48 - 2 * low) // 2, functools.partial(sweep, now, later, d))
+            over_rows(low, 48 - low, 48 - 2 * low, functools.partial(sweep, now, later, d))
             close(later)
             now, later = later, now
 
@@ -351,8 +351,6 @@
                 wave[a, 8 * half : 8 * half + 8, 128 * c : 128 * c + 128] = now[
                     a, pl.ds(8 * (16 + 8 * half) + c, 8, stride=8), :
                 ]
-    wave_copy = pltpu.make_async_copy(wave, wave_out, local_sem.at[0])
-    wave_copy.start()
 
     first_wait.wait_send()
     for copy in vhalos + z_own + x_own + c_own:
@@ -373,10 +371,6 @@
         for m in range(4):
             img[d, 4 * m : 4 * m + 4, :] = total[:, 32 * m : 32 * m + 32]
         done.wait_send()
-    img_copy = pltpu.make_async_copy(img, img_out, local_sem.at[1])
-    img_copy.start()
-    wave_copy.wait()
-    img_copy.wait()
 
 
 def solution(mesh):
@@ -388,11 +382,11 @@
         wave, image = pl.pallas_call(
             functools.partial(kernel, freqs, tiles),
             out_shape=[
-                jax.ShapeDtypeStruct((4, 16, 1024), f32),
-                jax.ShapeDtypeStruct((DEPTHS, 16, 32), f32),
+                pltpu.VMEM((4, 16, 1024), f32),
+                pltpu.VMEM((DEPTHS, 16, 32), f32),
             ],
             in_specs=[any_space] * 5,
-            out_specs=[any_space] * 2,
+            out_specs=[pl.BlockSpec(memory_space=pltpu.VMEM)] * 2,
             scratch_shapes=[
                 pltpu.VMEM((4, 16, 1024), f32),
                 pltpu.VMEM((16, 1024), f32),
@@ -408,8 +402,6 @@
                 pltpu.VMEM((18 * 8, 128), f32),
                 pltpu.VMEM((DEPTHS, 32 * 4, 128), f32),
                 pltpu.VMEM((DEPTHS, 32 * 4, 128), f32),
-                pltpu.VMEM((4, 16, 1024), f32),
-                pltpu.VMEM((DEPTHS, 16, 32), f32),
                 pltpu.SemaphoreType.DMA((5,)),
                 pltpu.SemaphoreType.DMA((2,)),
                 pltpu.SemaphoreType.DMA((2, len(CHUNKS), 8)),

time: 62.8 us -> 59 us (0.939)
  Pallas kernels: 59.4 us -> 56.9 us
  local copies, waits for them, and re-layouts: 2.3 us -> 1.32 us
    pallas_call x1, Pallas kernels: 59.4 us -> 56.9 us  [on_device(): pl.pallas_call(functools.partial(kernel, freqs, tiles), out_shape=[pltpu....]
    unnamed x4 -> x2, local copies, waits for them, and re-layouts: 2.3 us -> 1.32 us
where the time goes in v3:
time: 59 us; the launch traced here: 58.8 us
  Pallas kernels  56.9 us (96%)
  local copies, waits for them, and re-layouts  1.32 us (2%)
  between operations  0.64 us (1%)
    pallas_call x1, Pallas kernels, on_device(): pl.pallas_call(functools.partial(kernel, freqs, tiles), out_shape=[pltpu....  56.9 us
    unnamed x2, local copies, waits for them, and re-layouts  1.32 us

profile of v3, /device:TPU:1, one launch (start us, length us, event | category | flops | bytes accessed | tf_op | source)
XLA Modules:
  0.0 58.8 jit_solution(7419986004047452602)
XLA Ops:
  0.6 56.9 %shard_map.68 = (f32[4,16,1024]{2,1,0:T(8,128)S(1)}, f32[4,16,32]{2,1,0:T(8,128)S(1)}) custom-call(f32[2,16,1024]{2,1,0:T(8,128)} %bitcast.7, f32[2,16,1024]{2,1,0:T(8,128)} %bitcast.8, f32[16,1024]{1,0:T(8,128)} %bitcast.9, s32[4]{0:T(128)} %own.1, s32[16,32]{1,0:T(8,128)} %reg.1), custom_call_target="tpu_custom_call" | custom-call | tf_op jit(solution)/shard_map/pallas_call | solution.py:382
  57.5 0.7 %copy.10 = f32[2,2,1,16,1024]{4,3,2,1,0:T(8,128)} copy(f32[2,2,1,16,1024]{4,3,2,1,0:T(8,128)S(1)} %bitcast.6) | data formatting | bytes 524288
  58.2 0.6 %copy.11 = f32[4,16,32]{2,1,0:T(8,128)} copy(f32[4,16,32]{2,1,0:T(8,128)S(1)} %get-tuple-element.9) | data formatting | bytes 16384

commit v4 on v3

--- a/solution.py
+++ b/solution.py
@@ -55,8 +55,8 @@
     freqs, tiles,
     src, rcv, vel, own, reg,
     wave, img,
-    raw, velraw, regbuf, ownbuf, buf_a, buf_b, vels, stage, recv, labs, weights, imgb, pack, parts,
-    local_sem, first_sem, field_sem, vhalo_sem, z_sem, x_sem, core_sem, image_sem,
+    raw, velraw, regbuf, ownbuf, buf_a, buf_b, vels, stage, recv, label_in, labs, weights, imgb, pack, parts,
+    local_sem, first_sem, label_sem, field_sem, vhalo_sem, z_sem, x_sem, core_sem, image_sem,
 ):
     f = lax.axis_index("freq")
     t = lax.axis_index("tile")
@@ -98,9 +98,9 @@
     loads[1].wait()
     own_labels = regbuf[...].astype(jnp.float32) + 1.0
     own_labels = jnp.concatenate([own_labels[4 * m : 4 * m + 4] for m in range(4)], axis=1)
-    for j in range(32):
-        stage[8 * j + 4 : 8 * j + 8, :] = own_labels
-    mine = pl.ds(pl.multiple_of(8 * f, 8), 8)
+    held = pl.ds(pl.multiple_of(4 * (16 * core + row), 4), 4)
+    label_in[held, :] = own_labels
+    mine = pl.ds(pl.multiple_of(8 * f, 8), 4)
     recv[mine, :] = stage[mine, :]
     loads[3].wait()
     loads[4].wait()
@@ -117,7 +117,7 @@
     def first_send(i, carry):
         d = lax.rem(f + i, freqs)
         remote(
-            stage.at[pl.ds(pl.multiple_of(8 * d, 8), 8)],
+            stage.at[pl.ds(pl.multiple_of(8 * d, 8), 4)],
             recv.at[mine],
             first_sem.at[0],
             first_sem.at[1],
@@ -147,7 +147,7 @@
 
     send_fields(0)
 
-    bulk = pl.ds(0, 8 * (freqs - 1))
+    bulk = pl.ds(0, 4 * (freqs - 1))
     first_wait = remote(stage.at[bulk], recv.at[bulk], first_sem.at[0], first_sem.at[1], (f, after))
     first_wait.wait_recv()
     wanted = [jnp.full((8, 128), ownbuf[d], jnp.int32) for d in range(DEPTHS)]
@@ -188,6 +188,18 @@
     for copy in vhalos:
         copy.start()
     z_own = spread(1, row, 1, z_sem, z_peers)
+
+    def share(first, count, stage_no, peers):
+        piece = label_in.at[pl.ds(pl.multiple_of(4 * (16 * core + first), 4), 4 * count)]
+        copies = [
+            remote(piece, piece, label_sem.at[0, stage_no, i], label_sem.at[1, stage_no, i], peer)
+            for i, peer in enumerate(peers)
+        ]
+        for copy in copies:
+            copy.start()
+        return copies
+
+    label_z = share(row, 1, 0, z_peers)
     send_fields(1)
 
     lane = lax.broadcasted_iota(jnp.int32, (8, 128), 1)
@@ -202,8 +214,33 @@
         down = jnp.where(last_lane, ref[pl.ds(at - 1, 8), :], middle)
         return pltpu.roll(up, 127, 1), pltpu.roll(down, 1, 1)
 
+    for copy in z_own:
+        copy.wait_recv()
+    x_own = spread(1, 4 * xx, 4, x_sem, x_peers)
+    for copy in vhalos:
+        copy.wait_recv()
+    z_halo = [spread(part, row, 1, z_sem, z_peers) for part in (0, 2)]
+    send_fields(2)
+    for copy in label_z:
+        copy.wait_recv()
+    label_x = share(4 * xx, 4, 1, x_peers)
+    for copy in x_own:
+        copy.wait_recv()
+    c_own = spread(1, 0, 16, core_sem, [core_peer])
+    for copy in z_halo[0] + z_halo[1]:
+        copy.wait_recv()
+    x_halo = [spread(part, 4 * xx, 4, x_sem, x_peers) for part in (0, 2)]
+    send_fields(3)
+    for copy in label_x:
+        copy.wait_recv()
+    label_c = share(0, 16, 2, [core_peer])
+    for copy in x_halo[0] + x_halo[1]:
+        copy.wait_recv()
+    c_halo = [spread(part, 0, 16, core_sem, [core_peer]) for part in (0, 2)]
+    for copy in c_own + c_halo[0] + c_halo[1] + label_c:
+        copy.wait_recv()
     for i in range(4):
-        cols = [recv[pl.ds(8 * q + 4 + i, 8, stride=32), :] for q in range(4)]
+        cols = [label_in[pl.ds(64 * (q % 2) + 4 * (q // 2) + i, 8, stride=8), :] for q in range(4)]
         for m in range(4):
             total = None
             for q in range(4):
@@ -217,25 +254,6 @@
         weights[0, 8 * r : 8 * r + 8, :] = jnp.where((up == middle) & ~end_cell, scale, 0.0)
         weights[1, 8 * r : 8 * r + 8, :] = jnp.where((down == middle) & ~start_cell, scale, 0.0)
 
-    for copy in z_own:
-        copy.wait_recv()
-    x_own = spread(1, 4 * xx, 4, x_sem, x_peers)
-    for copy in vhalos:
-        copy.wait_recv()
-    z_halo = [spread(part, row, 1, z_sem, z_peers) for part in (0, 2)]
-    send_fields(2)
-    for copy in x_own:
-        copy.wait_recv()
-    c_own = spread(1, 0, 16, core_sem, [core_peer])
-    for copy in z_halo[0] + z_halo[1]:
-        copy.wait_recv()
-    x_halo = [spread(part, 4 * xx, 4, x_sem, x_peers) for part in (0, 2)]
-    send_fields(3)
-    for copy in x_halo[0] + x_halo[1]:
-        copy.wait_recv()
-    c_halo = [spread(part, 0, 16, core_sem, [core_peer]) for part in (0, 2)]
-    for copy in c_own + c_halo[0] + c_halo[1]:
-        copy.wait_recv()
     for copy in fields:
         copy.wait()
 
@@ -353,7 +371,7 @@
                 ]
 
     first_wait.wait_send()
-    for copy in vhalos + z_own + x_own + c_own:
+    for copy in vhalos + z_own + x_own + c_own + label_z + label_x + label_c:
         copy.wait_send()
     for group_of in (z_halo, x_halo, c_halo):
         for copy in group_of[0] + group_of[1]:
@@ -397,6 +415,7 @@
                 pltpu.VMEM((DEPTHS, 48, 8, 128), f32),
                 pltpu.VMEM((32 * 8, 128), f32),
                 pltpu.VMEM((32 * 8, 128), f32),
+                pltpu.VMEM((32 * 4, 128), f32),
                 pltpu.VMEM((18 * 8, 128), f32),
                 pltpu.VMEM((2, 16 * 8, 128), f32),
                 pltpu.VMEM((18 * 8, 128), f32),
@@ -404,6 +423,7 @@
                 pltpu.VMEM((DEPTHS, 32 * 4, 128), f32),
                 pltpu.SemaphoreType.DMA((5,)),
                 pltpu.SemaphoreType.DMA((2,)),
+                pltpu.SemaphoreType.DMA((2, 3, 3)),
                 pltpu.SemaphoreType.DMA((2, len(CHUNKS), 8)),
                 pltpu.SemaphoreType.DMA((2, 2)),
                 pltpu.SemaphoreType.DMA((2, 3, 3)),

time: 59 us -> 58.2 us (0.986)
  Pallas kernels: 56.9 us -> 56.1 us
    pallas_call x1, Pallas kernels: 56.9 us -> 56.1 us  [on_device(): pl.pallas_call(functools.partial(kernel, freqs, tiles), out_shape=[pltpu....]
where the time goes in v4:
time: 58.2 us; the launch traced here: 58.1 us
  Pallas kernels  56.1 us (96%)
  local copies, waits for them, and re-layouts  1.32 us (2%)
  between operations  0.64 us (1%)
    pallas_call x1, Pallas kernels, on_device(): pl.pallas_call(functools.partial(kernel, freqs, tiles), out_shape=[pltpu....  56.1 us
    unnamed x2, local copies, waits for them, and re-layouts  1.32 us

profile of v4, /device:TPU:1, one launch (start us, length us, event | category | flops | bytes accessed | tf_op | source)
XLA Modules:
  0.0 58.1 jit_solution(9494891880313041156)
XLA Ops:
  0.6 56.1 %shard_map.68 = (f32[4,16,1024]{2,1,0:T(8,128)S(1)}, f32[4,16,32]{2,1,0:T(8,128)S(1)}) custom-call(f32[2,16,1024]{2,1,0:T(8,128)} %bitcast.7, f32[2,16,1024]{2,1,0:T(8,128)} %bitcast.8, f32[16,1024]{1,0:T(8,128)} %bitcast.9, s32[4]{0:T(128)} %own.1, s32[16,32]{1,0:T(8,128)} %reg.1), custom_call_target="tpu_custom_call" | custom-call | tf_op jit(solution)/shard_map/pallas_call | solution.py:400
  56.7 0.7 %copy.10 = f32[2,2,1,16,1024]{4,3,2,1,0:T(8,128)} copy(f32[2,2,1,16,1024]{4,3,2,1,0:T(8,128)S(1)} %bitcast.6) | data formatting | bytes 524288
  57.4 0.6 %copy.11 = f32[4,16,32]{2,1,0:T(8,128)} copy(f32[4,16,32]{2,1,0:T(8,128)S(1)} %get-tuple-element.9) | data formatting | bytes 16384
